TPU v7x, 32 devices: a whole 2x2x4 slice. The times are simulated.
32 devices in a mesh: groups: 2 (over x), ctx: 16 (over z, y, core).
Axes of the slice: x: 2, y: 2, z: 4, core: 2. Of those that a mesh axis runs over, the one named last changes fastest.
Arguments:
- index_query: bfloat16 [512, 8192], P(('groups', 'ctx')), parts along dimension 0, may hold values from -4 to 4
- index_weight: float32 [512, 64], P(('groups', 'ctx')), parts along dimension 0, may hold values from -0.08 to 0.08
- index_keys: bfloat16 [8192, 128], P(('groups', 'ctx')), parts along dimension 0, may hold values from -4 to 4
- attn_query: bfloat16 [512, 128, 576], P(('groups', 'ctx')), parts along dimension 0, may hold values from -80 to 80
- latent_cache: bfloat16 [8192, 576], P(('groups', 'ctx')), parts along dimension 0, may hold values from -6 to 6
- positions: int32 [512], P(('groups', 'ctx')), parts along dimension 0, may hold values from 0 to 4095, as said below
- sel_keys: int32 [512, 2048], P(('groups', 'ctx')), parts along dimension 0, may hold values from 0 to 4095, as said below
- sel_count: int32 [512], P(('groups', 'ctx')), parts along dimension 0, may hold values from 1 to 1216, as said below
- page_slot: int32 [2048], P(('groups', 'ctx')), parts along dimension 0, may hold values from 0 to 1023, as said below
Outputs:
- index_scores: float32 [512, 4096], P(('groups', 'ctx')), parts along dimension 0
- attn_latent: bfloat16 [512, 128, 512], P(('groups', 'ctx')), parts along dimension 0
- decode_latent: bfloat16 [2048, 4, 576], P(('groups', 'ctx')), parts along dimension 0
- decode_index: bfloat16 [2048, 4, 128], P(('groups', 'ctx')), parts along dimension 0
There are 2 independent parts, one for each index of `groups`. A program takes and returns all parts, laid end to end along the dimension named above; each array names one. Nothing has to cross between parts.
Inputs may be any that keep to these rules, and one draw needn't show every extreme that they name: The 16 queries of device d sit at distinct rising positions among that device's rows d * 256 to d * 256 + 255, the last of them at the device's last row. `sel_keys`: row q lists sel_count[q] distinct rising key positions, none after positions[q] and one equal to it, then zeros. Among the keys named by the lists of one device's queries, at most 64 are rows of any one other device, and exactly 64 for some pair of devices in every draw. `sel_count`: the number of live slots in row q of sel_keys; the largest is reached in every draw. `page_slot`: A permutation. Slot s is held by device s // 64. The pages of one device go to 16 different devices, 4 to each, and every device receives 64 pages.
All inputs are finite; a program needn't handle non-finite values.
Results may differ from a plain program's by a relative error of at most 0.0047.
Values may be sent and summed in bfloat16 or wider, within the bound.
A program may use at most 128 MiB of HBM per device.

v0:
```python
import jax
import jax.numpy as jnp
from jax import lax
from jax.sharding import PartitionSpec as P

LAT = 512
PAGE = 4


neg_fill = -1e30
score_scale = 192.0 ** (-0.5)


def attend_query(one_query, key_rows, live_count):
    scores = (
        lax.dot_general(
            one_query, key_rows, (((1,), (1,)), ((), ())), preferred_element_type=jnp.float32
        )
        * score_scale
    )
    slot_ids = jnp.arange(key_rows.shape[0], dtype=jnp.int32)
    scores = jnp.where(slot_ids[None, :] < live_count, scores, neg_fill)
    highest = jnp.max(scores, axis=1, keepdims=True)
    lifted = jnp.exp(scores - highest)
    shares = (lifted / jnp.sum(lifted, axis=1, keepdims=True)).astype(jnp.bfloat16)
    return jnp.dot(shares, key_rows[:, :LAT], preferred_element_type=jnp.float32).astype(
        jnp.bfloat16
    )


def on_device(
    index_query,
    index_weight,
    index_keys,
    attn_query,
    latent_cache,
    positions,
    sel_keys,
    sel_count,
    page_slot,
):
    members = lax.axis_size("ctx")
    local_rows = latent_cache.shape[0]
    queries = index_query.shape[0]
    index_heads = index_weight.shape[1]
    head_width = index_keys.shape[1]
    query_heads = index_query.reshape(queries * index_heads, head_width)

    def score_block(segment, offset):
        raw = lax.dot_general(
            query_heads, segment, (((1,), (1,)), ((), ())), preferred_element_type=jnp.float32
        )
        raw = jnp.maximum(raw, 0.0).reshape(queries, index_heads, segment.shape[0])
        summed = jnp.sum(raw * index_weight[:, :, None], axis=1)
        columns = offset + jnp.arange(segment.shape[0], dtype=jnp.int32)
        return jnp.where(columns[None, :] <= positions[:, None], summed, 0.0)

    segment = lax.all_gather(index_keys, "ctx", axis=0, tiled=True)
    seg_rows = segment.shape[0]
    width_block = 1024
    blocks = segment.reshape(seg_rows // width_block, width_block, head_width)
    starts = width_block * jnp.arange(seg_rows // width_block, dtype=jnp.int32)
    block_scores = lax.map(
        lambda entry_pair: score_block(entry_pair[0], entry_pair[1]), (blocks, starts)
    )
    index_scores = jnp.moveaxis(block_scores, 0, 1).reshape(queries, seg_rows)
    key_table = lax.all_gather(latent_cache, "ctx", axis=0, tiled=True)

    def attend_entry(entry):
        return attend_query(entry[0], key_table[entry[1]], entry[2])

    attn_latent = lax.map(attend_entry, (attn_query, sel_keys, sel_count))
    page_count = local_rows // PAGE
    capacity = max(1, page_count // members)
    owners = page_slot // page_count
    page_ids = jnp.arange(page_count, dtype=jnp.int32)
    earlier = (owners[:, None] == owners[None, :]) & (page_ids[None, :] < page_ids[:, None])
    order_in = jnp.sum(earlier.astype(jnp.int32), axis=1)
    latent_pages = latent_cache.reshape(page_count, PAGE, latent_cache.shape[1])
    index_pages = index_keys.reshape(page_count, PAGE, head_width)
    send_latent = (
        jnp.zeros((members, capacity) + latent_pages.shape[1:], jnp.bfloat16)
        .at[owners, order_in]
        .set(latent_pages)
    )
    send_index = (
        jnp.zeros((members, capacity) + index_pages.shape[1:], jnp.bfloat16)
        .at[owners, order_in]
        .set(index_pages)
    )
    send_slots = jnp.full((members, capacity), -1, jnp.int32).at[owners, order_in].set(page_slot)
    got_latent, got_index, got_slots = (
        lax.all_to_all(send_latent, "ctx", split_axis=0, concat_axis=0, tiled=True),
        lax.all_to_all(send_index, "ctx", split_axis=0, concat_axis=0, tiled=True),
        lax.all_to_all(send_slots, "ctx", split_axis=0, concat_axis=0, tiled=True),
    )
    places = jnp.where(got_slots >= 0, got_slots % page_count, page_count).reshape(-1)
    decode_latent = (
        jnp.zeros(latent_pages.shape, jnp.bfloat16)
        .at[places]
        .set(got_latent.reshape((-1,) + latent_pages.shape[1:]), mode="drop")
    )
    decode_index = (
        jnp.zeros(index_pages.shape, jnp.bfloat16)
        .at[places]
        .set(got_index.reshape((-1,) + index_pages.shape[1:]), mode="drop")
    )
    return (index_scores, attn_latent, decode_latent, decode_index)


def solution(mesh):
    in_specs = (
        P(("groups", "ctx"), None),
        P(("groups", "ctx"), None),
        P(("groups", "ctx"), None),
        P(("groups", "ctx"), None, None),
        P(("groups", "ctx"), None),
        P(("groups", "ctx")),
        P(("groups", "ctx"), None),
        P(("groups", "ctx")),
        P(("groups", "ctx")),
    )
    out_specs = (
        P(("groups", "ctx"), None),
        P(("groups", "ctx"), None, None),
        P(("groups", "ctx"), None, None),
        P(("groups", "ctx"), None, None),
    )
    return jax.shard_map(
        on_device, mesh=mesh, in_specs=in_specs, out_specs=out_specs, check_vma=False
    )
```

profile of v0, /device:TPU:1, one launch (start us, length us, event | category | flops | bytes accessed | tf_op | source)
XLA Modules:
  0.0 386.5 jit_solution(11782332921097171760)
XLA Ops:
  11.4 5.8 %scatter_fusion = s32[16,4]{0,1:T(4,128)S(1)} fusion(s32[16,4]{0,1:T(4,128)S(1)} %broadcast_in_dim.69, s32[64]{0:T(128)S(1)} %fusion.27, s32[64]{0:T(128)} %param.21), kind=kCustom, calls=%fused_computation.1 | custom fusion | bytes 1280 | tf_op jit(solution)/shard_map/scatter | solution.py:91
  17.8 7.5 %all-to-all-start = ((s32[16,1,4]{2,1,0:T(1,128)}), s32[16,1,4]{2,1,0:T(1,128)S(1)}, u32[]{:S(2)}, u32[]{:S(2)}) async-start(s32[16,1,4]{2,1,0:T(1,128)} %copy.27), calls=%async_computation | async-start | bytes 16384 | tf_op jit(solution)/shard_map/all_to_all | solution.py:95
  26.0 7.8 %scatter_fusion.3 = bf16[16,4,4,128]{3,2,1,0:T(4,128)(2,1)} fusion(bf16[16,4,4,128]{3,2,1,0:T(4,128)(2,1)} %broadcast_in_dim.73, s32[64]{0:T(128)S(1)} %fusion.27, bf16[64,4,128]{2,1,0:T(4,128)(2,1)} %bitcast.76), kind=kCustom, calls=%fused_computation.4 | custom fusion | bytes 197120 | tf_op jit(solution)/shard_map/scatter | solution.py:89
  33.8 6.0 %all-to-all-start.2 = ((bf16[16,4,4,128]{3,2,1,0:T(4,128)(2,1)}), bf16[16,4,4,128]{3,2,1,0:T(4,128)(2,1)S(1)}, u32[]{:S(2)}, u32[]{:S(2)}) async-start(bf16[16,4,4,128]{3,2,1,0:T(4,128)(2,1)} %scatter_fusion.3), calls=%async_computation.2 | async-start | bytes 131072 | tf_op jit(solution)/shard_map/all_to_all | solution.py:94
  41.7 8.6 %scatter_fusion.1 = bf16[16,4,4,576]{3,2,1,0:T(4,128)(2,1)} fusion(bf16[16,4,4,576]{3,2,1,0:T(4,128)(2,1)} %broadcast_in_dim.71, s32[64]{0:T(128)S(1)} %fusion.27, bf16[64,4,576]{2,1,0:T(4,128)(2,1)S(1)} %reshape.236), kind=kCustom, calls=%fused_computation.2 | custom fusion | bytes 885248 | tf_op jit(solution)/shard_map/scatter | solution.py:84
  50.3 6.0 %all-to-all-start.1 = ((bf16[16,4,4,576]{3,2,1,0:T(4,128)(2,1)}), bf16[16,4,4,576]{3,2,1,0:T(4,128)(2,1)S(1)}, u32[]{:S(2)}, u32[]{:S(2)}) async-start(bf16[16,4,4,576]{3,2,1,0:T(4,128)(2,1)} %scatter_fusion.1), calls=%async_computation.1 | async-start | bytes 655360 | tf_op jit(solution)/shard_map/all_to_all | solution.py:93
  57.8 2.4 scatter_fusion.4
  60.3 8.4 %all-to-all-done.1 = bf16[16,4,4,576]{3,2,1,0:T(4,128)(2,1)S(1)} async-done(((bf16[16,4,4,576]{3,2,1,0:T(4,128)(2,1)}), bf16[16,4,4,576]{3,2,1,0:T(4,128)(2,1)S(1)}, u32[]{:S(2)}, u32[]{:S(2)}) %all-to-all-start.1) | async-done | bytes 294944 | tf_op jit(solution)/shard_map/all_to_all | solution.py:93
  68.7 2.5 scatter_fusion.2
  72.0 12.1 %while.20 = (s32[]{:T(128)}, f32[4,16,1024]{2,1,0:T(8,128)S(1)}, s32[4]{0:T(128)S(1)}, s32[16]{0:T(128)S(1)}, bf16[4,1024,128]{2,1,0:T(8,128)(2,1)}, /*index=5*/...) while((s32[]{:T(128)}, f32[4,16,1024]{2,1,0:T(8,128)S(1)}, s32[4]{0:T(128)S(1)}, s32[16]{0:T(128)S(1)}, ...), condition=%wide.region_2.3_spmd, body=%wide.region_0.2_spmd.sunk | while | flops 271598592 | bytes 734313 | solution.py:63
  84.8 26.7 %all-gather.5.cloned.1.call-done = bf16[4096,576]{1,0:T(8,128)(2,1)} async-done(((bf16[256,576]{1,0:T(8,128)(2,1)}), bf16[4096,576]{1,0:T(8,128)(2,1)}) %all-gather.5.cloned.1.call-update) | async-done | bytes 4718608 | tf_op jit(solution)/shard_map/all_gather | solution.py:67
  111.5 268.1 %while.21 = (s32[]{:T(128)}, bf16[16,128,512]{2,1,0:T(8,128)(2,1)}, s32[16]{0:T(128)S(1)}, bf16[16,128,576]{1,2,0:T(8,128)(2,1)}, s32[16,2048]{1,0:T(8,128)}, /*index=5*/bf16[4096,576]{1,0:T(8,128)(2,1)}, s32[]{:T(128)}) while((s32[]{:T(128)}, bf16[16,128,512]{2,1,0:T(8,128)(2,1)}, s32[16]{0:T(128)S(1)}, bf16[16,128,576]{1,2,0:T(8,128)(2,1)}, ...), condition=%wide.region_6.7_spmd, body=%wide.region_3.6_spmd.sunk | while | flops 572598016 | bytes 12648033 | solution.py:72
  112.4 11.1 %gather_fusion = bf16[2048,576]{1,0:T(8,128)(2,1)S(1)} fusion(bf16[4096,576]{1,0:T(8,128)(2,1)} %get-tuple-element.230, s32[2048]{0:T(1024)S(1)} %broadcast_clamp_fusion.2), kind=kCustom, calls=%fused_computation.clone.1 | custom fusion | bytes 4726784 | tf_op jit(solution)/shard_map/while/body/eval_jaxpr/gather | solution.py:70
  129.2 11.1 %gather_fusion = bf16[2048,576]{1,0:T(8,128)(2,1)S(1)} fusion(bf16[4096,576]{1,0:T(8,128)(2,1)} %get-tuple-element.230, s32[2048]{0:T(1024)S(1)} %broadcast_clamp_fusion.2), kind=kCustom, calls=%fused_computation.clone.1 | custom fusion | bytes 4726784 | tf_op jit(solution)/shard_map/while/body/eval_jaxpr/gather | solution.py:70
  145.9 11.1 %gather_fusion = bf16[2048,576]{1,0:T(8,128)(2,1)S(1)} fusion(bf16[4096,576]{1,0:T(8,128)(2,1)} %get-tuple-element.230, s32[2048]{0:T(1024)S(1)} %broadcast_clamp_fusion.2), kind=kCustom, calls=%fused_computation.clone.1 | custom fusion | bytes 4726784 | tf_op jit(solution)/shard_map/while/body/eval_jaxpr/gather | solution.py:70
  158.3 2.0 fusion.42
  162.7 11.1 %gather_fusion = bf16[2048,576]{1,0:T(8,128)(2,1)S(1)} fusion(bf16[4096,576]{1,0:T(8,128)(2,1)} %get-tuple-element.230, s32[2048]{0:T(1024)S(1)} %broadcast_clamp_fusion.2), kind=kCustom, calls=%fused_computation.clone.1 | custom fusion | bytes 4726784 | tf_op jit(solution)/shard_map/while/body/eval_jaxpr/gather | solution.py:70
  175.1 2.0 fusion.42
  179.4 11.1 %gather_fusion = bf16[2048,576]{1,0:T(8,128)(2,1)S(1)} fusion(bf16[4096,576]{1,0:T(8,128)(2,1)} %get-tuple-element.230, s32[2048]{0:T(1024)S(1)} %broadcast_clamp_fusion.2), kind=kCustom, calls=%fused_computation.clone.1 | custom fusion | bytes 4726784 | tf_op jit(solution)/shard_map/while/body/eval_jaxpr/gather | solution.py:70
  191.8 2.0 fusion.42
  196.2 11.1 %gather_fusion = bf16[2048,576]{1,0:T(8,128)(2,1)S(1)} fusion(bf16[4096,576]{1,0:T(8,128)(2,1)} %get-tuple-element.230, s32[2048]{0:T(1024)S(1)} %broadcast_clamp_fusion.2), kind=kCustom, calls=%fused_computation.clone.1 | custom fusion | bytes 4726784 | tf_op jit(solution)/shard_map/while/body/eval_jaxpr/gather | solution.py:70
  213.0 11.1 %gather_fusion = bf16[2048,576]{1,0:T(8,128)(2,1)S(1)} fusion(bf16[4096,576]{1,0:T(8,128)(2,1)} %get-tuple-element.230, s32[2048]{0:T(1024)S(1)} %broadcast_clamp_fusion.2), kind=kCustom, calls=%fused_computation.clone.1 | custom fusion | bytes 4726784 | tf_op jit(solution)/shard_map/while/body/eval_jaxpr/gather | solution.py:70
  225.3 2.0 fusion.42
  229.7 11.1 %gather_fusion = bf16[2048,576]{1,0:T(8,128)(2,1)S(1)} fusion(bf16[4096,576]{1,0:T(8,128)(2,1)} %get-tuple-element.230, s32[2048]{0:T(1024)S(1)} %broadcast_clamp_fusion.2), kind=kCustom, calls=%fused_computation.clone.1 | custom fusion | bytes 4726784 | tf_op jit(solution)/shard_map/while/body/eval_jaxpr/gather | solution.py:70
  246.5 11.1 %gather_fusion = bf16[2048,576]{1,0:T(8,128)(2,1)S(1)} fusion(bf16[4096,576]{1,0:T(8,128)(2,1)} %get-tuple-element.230, s32[2048]{0:T(1024)S(1)} %broadcast_clamp_fusion.2), kind=kCustom, calls=%fused_computation.clone.1 | custom fusion | bytes 4726784 | tf_op jit(solution)/shard_map/while/body/eval_jaxpr/gather | solution.py:70
  263.2 11.1 %gather_fusion = bf16[2048,576]{1,0:T(8,128)(2,1)S(1)} fusion(bf16[4096,576]{1,0:T(8,128)(2,1)} %get-tuple-element.230, s32[2048]{0:T(1024)S(1)} %broadcast_clamp_fusion.2), kind=kCustom, calls=%fused_computation.clone.1 | custom fusion | bytes 4726784 | tf_op jit(solution)/shard_map/while/body/eval_jaxpr/gather | solution.py:70
  280.0 11.1 %gather_fusion = bf16[2048,576]{1,0:T(8,128)(2,1)S(1)} fusion(bf16[4096,576]{1,0:T(8,128)(2,1)} %get-tuple-element.230, s32[2048]{0:T(1024)S(1)} %broadcast_clamp_fusion.2), kind=kCustom, calls=%fused_computation.clone.1 | custom fusion | bytes 4726784 | tf_op jit(solution)/shard_map/while/body/eval_jaxpr/gather | solution.py:70
  296.7 11.1 %gather_fusion = bf16[2048,576]{1,0:T(8,128)(2,1)S(1)} fusion(bf16[4096,576]{1,0:T(8,128)(2,1)} %get-tuple-element.230, s32[2048]{0:T(1024)S(1)} %broadcast_clamp_fusion.2), kind=kCustom, calls=%fused_computation.clone.1 | custom fusion | bytes 4726784 | tf_op jit(solution)/shard_map/while/body/eval_jaxpr/gather | solution.py:70
  313.5 11.1 %gather_fusion = bf16[2048,576]{1,0:T(8,128)(2,1)S(1)} fusion(bf16[4096,576]{1,0:T(8,128)(2,1)} %get-tuple-element.230, s32[2048]{0:T(1024)S(1)} %broadcast_clamp_fusion.2), kind=kCustom, calls=%fused_computation.clone.1 | custom fusion | bytes 4726784 | tf_op jit(solution)/shard_map/while/body/eval_jaxpr/gather | solution.py:70
  330.3 11.1 %gather_fusion = bf16[2048,576]{1,0:T(8,128)(2,1)S(1)} fusion(bf16[4096,576]{1,0:T(8,128)(2,1)} %get-tuple-element.230, s32[2048]{0:T(1024)S(1)} %broadcast_clamp_fusion.2), kind=kCustom, calls=%fused_computation.clone.1 | custom fusion | bytes 4726784 | tf_op jit(solution)/shard_map/while/body/eval_jaxpr/gather | solution.py:70
  347.0 11.1 %gather_fusion = bf16[2048,576]{1,0:T(8,128)(2,1)S(1)} fusion(bf16[4096,576]{1,0:T(8,128)(2,1)} %get-tuple-element.230, s32[2048]{0:T(1024)S(1)} %broadcast_clamp_fusion.2), kind=kCustom, calls=%fused_computation.clone.1 | custom fusion | bytes 4726784 | tf_op jit(solution)/shard_map/while/body/eval_jaxpr/gather | solution.py:70
  363.8 11.1 %gather_fusion = bf16[2048,576]{1,0:T(8,128)(2,1)S(1)} fusion(bf16[4096,576]{1,0:T(8,128)(2,1)} %get-tuple-element.230, s32[2048]{0:T(1024)S(1)} %broadcast_clamp_fusion.2), kind=kCustom, calls=%fused_computation.clone.1 | custom fusion | bytes 4726784 | tf_op jit(solution)/shard_map/while/body/eval_jaxpr/gather | solution.py:70
  (163 shorter events, 104.2 us)
Async XLA Ops:
  7.2 49.2 %copy-start.2 = (bf16[16,8192]{1,0:T(8,128)(2,1)S(1)}, bf16[16,8192]{1,0:T(8,128)(2,1)}, u32[]{:S(2)}) copy-start(bf16[16,8192]{1,0:T(8,128)(2,1)} %param.13) | copy-start | bytes 786436
  7.2 64.1 %all-gather.3.cloned.1.call-start = ((), (), s32[]{:S(2)}) async-start(), calls=%async_computation.3 | async-start | bytes 1114112 | tf_op jit(solution)/shard_map/all_gather | solution.py:58
  7.9 103.6 %all-gather.5.cloned.1.call-start = ((), (), s32[]{:S(2)}) async-start(), calls=%async_computation.4 | async-start | bytes 5570560 | tf_op jit(solution)/shard_map/all_gather | solution.py:67
  17.8 53.5 %copy-start.3 = (s32[16]{0:T(128)S(1)}, s32[16]{0:T(128)}, u32[]{:S(2)}) copy-start(s32[16]{0:T(128)} %param.18) | copy-start | bytes 196
  17.8 53.5 %copy-start.4 = (f32[16,64]{1,0:T(8,128)S(1)}, f32[16,64]{1,0:T(8,128)}, u32[]{:S(2)}) copy-start(f32[16,64]{1,0:T(8,128)} %param.14) | copy-start | bytes 12292
  17.8 15.9 %all-to-all-start = ((s32[16,1,4]{2,1,0:T(1,128)}), s32[16,1,4]{2,1,0:T(1,128)S(1)}, u32[]{:S(2)}, u32[]{:S(2)}) async-start(s32[16,1,4]{2,1,0:T(1,128)} %copy.27), calls=%async_computation | async-start | bytes 16384 | tf_op jit(solution)/shard_map/all_to_all | solution.py:95
  33.8 16.5 %all-to-all-start.2 = ((bf16[16,4,4,128]{3,2,1,0:T(4,128)(2,1)}), bf16[16,4,4,128]{3,2,1,0:T(4,128)(2,1)S(1)}, u32[]{:S(2)}, u32[]{:S(2)}) async-start(bf16[16,4,4,128]{3,2,1,0:T(4,128)(2,1)} %scatter_fusion.3), calls=%async_computation.2 | async-start | bytes 131072 | tf_op jit(solution)/shard_map/all_to_all | solution.py:94
  50.3 18.3 %all-to-all-start.1 = ((bf16[16,4,4,576]{3,2,1,0:T(4,128)(2,1)}), bf16[16,4,4,576]{3,2,1,0:T(4,128)(2,1)S(1)}, u32[]{:S(2)}, u32[]{:S(2)}) async-start(bf16[16,4,4,576]{3,2,1,0:T(4,128)(2,1)} %scatter_fusion.1), calls=%async_computation.1 | async-start | bytes 655360 | tf_op jit(solution)/shard_map/all_to_all | solution.py:93
  60.2 11.1 %copy-start.1 = (bf16[64,4,128]{2,1,0:T(4,128)(2,1)}, bf16[64,4,128]{2,1,0:T(4,128)(2,1)S(1)}, u32[]{:S(2)}) copy-start(bf16[64,4,128]{2,1,0:T(4,128)(2,1)S(1)} %scatter_fusion.4) | copy-start | bytes 196612
  71.3 0.7 copy-start
  71.3 40.2 %copy-start.5 = (s32[16]{0:T(128)S(1)}, s32[16]{0:T(128)}, u32[]{:S(2)}) copy-start(s32[16]{0:T(128)} %param.20) | copy-start | bytes 196
Sparse Core Ops, SparseCore 0:
  10.2 40.5 all-gather.2
  53.0 58.4 all-gather.4
where the time goes:
time: 390 us; the launch traced here: 387 us
  local copies, waits for them, and re-layouts  225 us (58%)
  matrix products  57.9 us (15%)
  waiting for transfers between devices  35.8 us (9%)
  other arithmetic  33.9 us (9%)
  starting transfers between devices  19.6 us (5%)
  between operations  14.2 us (4%)
    gather x16, local copies, waits for them, and re-layouts, attend_entry(): return attend_query(entry[0], key_table[entry[1]], entry[2])  178 us
    dot_general x16, matrix products, attend_query(): lax.dot_general(one_query, key_rows, (((1,), (1,)), ((), ())), preferred_...  32 us
    all_gather x1, waiting for transfers between devices, on_device(): key_table = lax.all_gather(latent_cache, 'ctx', axis=0, tiled=True)  26.7 us
    dot_general x16, matrix products, attend_query(): jnp.dot(shares, key_rows[:, :LAT], preferred_element_type=jnp.float32)  19.2 us
    select_n x16, other arithmetic, attend_entry(): return attend_query(entry[0], key_table[entry[1]], entry[2])  13.7 us
    lt x16, other arithmetic, attend_query(): scores = jnp.where(slot_ids[None, :] < live_count, scores, neg_fill)  10.2 us
    dynamic_slice x16, local copies, waits for them, and re-layouts, on_device(): attn_latent = lax.map(attend_entry, (attn_query, sel_keys, sel_count))  9.84 us
    scatter x1, local copies, waits for them, and re-layouts, on_device(): send_latent = jnp.zeros((members, capacity) + latent_pages.shape[1:], jnp...  8.64 us
  transfers between devices with their start and end apart: 5, of which 2 were waited for; matrix products, arithmetic and copies ran while one was open for 12% of the time, Pallas kernels for 0%

commit v1 on v0

v1 whole, which is shorter than its diff:
```python
import functools
import math

import jax
import jax.numpy as jnp
from jax import lax
from jax.experimental import pallas as pl
from jax.experimental.pallas import tpu as pltpu
from jax.sharding import PartitionSpec as P

LAT = 512
PAGE = 4
FETCH = 64
LANES = 128
neg_fill = -1e30
score_scale = 192.0 ** (-0.5)
NT = (((1,), (1,)), ((), ()))


def prepare_kernel(members, local_rows, me_ref, keys_ref, count_ref, pick_ref, bias_ref, marks):
    me = me_ref[0]
    queries, slots = keys_ref.shape
    blocks = members * local_rows // LANES
    per = local_rows // LANES

    def mark(q, carry):
        keys = keys_ref[pl.ds(q, 1), :]
        live = lax.broadcasted_iota(jnp.int32, (1, slots), 1) < count_ref[q]
        keys = jnp.where(live, keys, -1)
        high = jnp.broadcast_to(keys >> 7, (blocks, slots))
        low = jnp.broadcast_to(keys & 127, (LANES, slots))
        in_block = (high == lax.broadcasted_iota(jnp.int32, (blocks, slots), 0)).astype(jnp.bfloat16)
        in_lane = (low == lax.broadcasted_iota(jnp.int32, (LANES, slots), 0)).astype(jnp.bfloat16)
        marks[:, pl.ds(q, 1), :] = lax.dot_general(
            in_block, in_lane, NT, preferred_element_type=jnp.float32
        ).reshape(blocks, 1, LANES)
        return carry

    lax.fori_loop(0, queries, mark, 0)

    def owner_marks(owner):
        return jnp.concatenate([marks[owner * per + k] for k in range(per)], axis=1)

    before = (
        lax.broadcasted_iota(jnp.int32, (local_rows, local_rows), 0)
        < lax.broadcasted_iota(jnp.int32, (local_rows, local_rows), 1)
    ).astype(jnp.bfloat16)
    place = lax.broadcasted_iota(jnp.int32, (FETCH, local_rows), 0).astype(jnp.float32)

    def compact(owner):
        own = owner_marks(owner)
        used = jnp.max(own, axis=0, keepdims=True)
        used = jnp.where(me == owner, 0.0, used)
        rank = jnp.dot(
            jnp.broadcast_to(used, (16, local_rows)).astype(jnp.bfloat16),
            before,
            preferred_element_type=jnp.float32,
        )[:1]
        rank = jnp.where(used > 0.5, rank, -1.0)
        pick = (jnp.broadcast_to(rank, (FETCH, local_rows)) == place).astype(jnp.bfloat16)
        return pick, lax.dot_general(
            own.astype(jnp.bfloat16), pick, NT, preferred_element_type=jnp.float32
        )

    for pair in range(members // 2):
        pick_a, named_a = compact(2 * pair)
        pick_b, named_b = compact(2 * pair + 1)
        pick_ref[2 * pair] = pick_a
        pick_ref[2 * pair + 1] = pick_b
        named = jnp.concatenate([named_a, named_b], axis=1)
        bias_ref[:, pair * LANES : (pair + 1) * LANES] = jnp.where(named > 0.5, 0.0, neg_fill)
    bias_ref[:, members * FETCH :] = jnp.where(owner_marks(me) > 0.5, 0.0, neg_fill)


def index_kernel(heads, query_ref, weight_ref, keys_ref, place_ref, out_ref, stacked, spread):
    queries = query_ref.shape[0]
    width = keys_ref.shape[1]
    step = 512
    for h in range(heads):
        stacked[h * queries : (h + 1) * queries, :] = query_ref[:, h * width : (h + 1) * width]
        spread[h * queries : (h + 1) * queries, :] = jnp.broadcast_to(
            weight_ref[:, h : h + 1], (queries, LANES)
        )
    places = jnp.broadcast_to(place_ref[...], (queries, step))
    group = 16

    def block(b, carry):
        start = pl.multiple_of(b * step, step)
        keys = keys_ref[pl.ds(start, step), :]
        total = jnp.zeros((queries, step), jnp.float32)
        for g in range(heads // group):
            rows = slice(g * group * queries, (g + 1) * group * queries)
            raw = lax.dot_general(stacked[rows, :], keys, NT, preferred_element_type=jnp.float32)
            raw = jnp.maximum(raw, 0.0)
            for k in range(group):
                weight = spread[(g * group + k) * queries : (g * group + k + 1) * queries, :]
                total = total + raw[k * queries : (k + 1) * queries] * jnp.concatenate(
                    [weight] * (step // LANES), axis=1
                )
        columns = start + lax.broadcasted_iota(jnp.int32, (queries, step), 1)
        out_ref[:, pl.ds(start, step)] = jnp.where(columns <= places, total, 0.0)
        return carry

    lax.fori_loop(0, keys_ref.shape[0] // step, block, 0)


def attend_kernel(
    members, group, me_ref, slot_ref, pick_ref, bias_ref, query_ref, table_ref, index_ref,
    out_ref, latent_out, index_out, chosen, onehot,
):
    me = me_ref[0]
    local_rows = table_ref.shape[0] // members
    queries, heads, row = query_ref.shape

    def bring(owner, carry):
        source = table_ref[pl.ds(pl.multiple_of(owner * local_rows, local_rows), local_rows), :]
        chosen[pl.ds(pl.multiple_of(owner * FETCH, FETCH), FETCH), :] = jnp.dot(
            pick_ref[owner], source, preferred_element_type=jnp.float32
        ).astype(jnp.bfloat16)
        return carry

    lax.fori_loop(0, members, bring, 0)
    chosen[members * FETCH :, :] = table_ref[
        pl.ds(pl.multiple_of(me * local_rows, local_rows), local_rows), :
    ]

    factor = score_scale * math.log2(math.e)

    def attend(g, carry):
        query = query_ref[pl.ds(g * group, group)].reshape(group * heads, row)
        scores = lax.dot_general(query, chosen[...], NT, preferred_element_type=jnp.float32)
        shares, sums = [], []
        for k in range(group):
            part = scores[k * heads : (k + 1) * heads] + bias_ref[pl.ds(g * group + k, 1), :]
            highest = jnp.max(part, axis=1, keepdims=True)
            lifted = jnp.exp2((part - highest) * factor)
            sums.append(jnp.sum(lifted, axis=1, keepdims=True))
            shares.append(lifted.astype(jnp.bfloat16))
        total = jnp.dot(
            jnp.concatenate(shares, axis=0), chosen[:, :LAT], preferred_element_type=jnp.float32
        )
        total = total / jnp.concatenate(sums, axis=0)
        out_ref[pl.ds(g * group, group)] = total.astype(jnp.bfloat16).reshape(group, heads, LAT)
        return carry

    lax.fori_loop(0, queries // group, attend, 0)

    target = me * local_rows + lax.broadcasted_iota(jnp.int32, (local_rows, local_rows), 0)

    def route(owner, carry):
        start = pl.multiple_of(owner * local_rows, local_rows)
        slots = jnp.broadcast_to(slot_ref[:, pl.ds(start, local_rows)], (local_rows, local_rows))
        onehot[:, pl.ds(start, local_rows)] = (slots == target).astype(jnp.bfloat16)
        return carry

    lax.fori_loop(0, members, route, 0)
    latent_out[...] = jnp.dot(
        onehot[...], table_ref[...], preferred_element_type=jnp.float32
    ).astype(jnp.bfloat16)
    index_out[...] = jnp.dot(
        onehot[...], index_ref[...], preferred_element_type=jnp.float32
    ).astype(jnp.bfloat16)


VMEM = pl.BlockSpec(memory_space=pltpu.VMEM)
SMEM = pl.BlockSpec(memory_space=pltpu.SMEM)


def on_device(
    index_query, index_weight, index_keys, attn_query, latent_cache, positions, sel_keys,
    sel_count, page_slot,
):
    members = lax.axis_size("ctx")
    local_rows, row = latent_cache.shape
    queries, index_heads = index_weight.shape
    head_width = index_keys.shape[1]
    attn_heads = attn_query.shape[1]
    total_rows = members * local_rows
    columns = members * FETCH + local_rows
    params = pltpu.CompilerParams(vmem_limit_bytes=60 * 2**20)
    me = lax.axis_index("ctx").reshape(1).astype(jnp.int32)

    row_slot = (page_slot[:, None] * PAGE + jnp.arange(PAGE, dtype=jnp.int32)[None, :]).reshape(1, -1)
    all_index = lax.all_gather(index_keys, "ctx", axis=0, tiled=True)
    table = lax.all_gather(latent_cache, "ctx", axis=0, tiled=True)
    all_slots = lax.all_gather(row_slot, "ctx", axis=1, tiled=True)

    pick, bias = pl.pallas_call(
        functools.partial(prepare_kernel, members, local_rows),
        out_shape=(
            jax.ShapeDtypeStruct((members, FETCH, local_rows), jnp.bfloat16),
            jax.ShapeDtypeStruct((queries, columns), jnp.float32),
        ),
        in_specs=[SMEM, VMEM, SMEM],
        out_specs=(VMEM, VMEM),
        scratch_shapes=[pltpu.VMEM((total_rows // LANES, queries, LANES), jnp.float32)],
        compiler_params=params,
        cost_estimate=pl.CostEstimate(flops=10**9, bytes_accessed=10**7, transcendentals=0),
        name="prepare",
    )(me, sel_keys, sel_count)

    index_scores = pl.pallas_call(
        functools.partial(index_kernel, index_heads),
        out_shape=jax.ShapeDtypeStruct((queries, total_rows), jnp.float32),
        in_specs=[VMEM] * 4,
        out_specs=VMEM,
        scratch_shapes=[
            pltpu.VMEM((index_heads * queries, head_width), jnp.bfloat16),
            pltpu.VMEM((index_heads * queries, LANES), jnp.float32),
        ],
        compiler_params=params,
        cost_estimate=pl.CostEstimate(flops=10**9, bytes_accessed=2 * 10**7, transcendentals=0),
        name="index_scores",
    )(index_query, index_weight, all_index, positions[:, None])

    attn_latent, decode_latent, decode_index = pl.pallas_call(
        functools.partial(attend_kernel, members, 4 if columns <= 2048 else 2),
        out_shape=(
            jax.ShapeDtypeStruct((queries, attn_heads, LAT), jnp.bfloat16),
            jax.ShapeDtypeStruct((local_rows, row), jnp.bfloat16),
            jax.ShapeDtypeStruct((local_rows, head_width), jnp.bfloat16),
        ),
        in_specs=[SMEM] + [VMEM] * 6,
        out_specs=(VMEM,) * 3,
        scratch_shapes=[
            pltpu.VMEM((columns, row), jnp.bfloat16),
            pltpu.VMEM((local_rows, total_rows), jnp.bfloat16),
        ],
        compiler_params=params,
        name="attend",
    )(me, all_slots, pick, bias, attn_query, table, all_index)
    return (
        index_scores,
        attn_latent,
        decode_latent.reshape(local_rows // PAGE, PAGE, row),
        decode_index.reshape(local_rows // PAGE, PAGE, head_width),
    )


def solution(mesh):
    rows = P(("groups", "ctx"), None)
    deep = P(("groups", "ctx"), None, None)
    flat = P(("groups", "ctx"))
    return jax.shard_map(
        on_device,
        mesh=mesh,
        in_specs=(rows, rows, rows, deep, rows, flat, rows, flat, flat),
        out_specs=(rows, deep, deep, deep),
        check_vma=False,
    )
```

time: 390 us -> 137 us (0.35)
  local copies, waits for them, and re-layouts: 225 us -> 8.81 us
  matrix products: 57.9 us -> 0 us
  Pallas kernels: 0 us -> 34.1 us
  other arithmetic: 33.9 us -> 0.08 us
  blocking collectives: 0 us -> 24 us
  starting transfers between devices: 19.6 us -> 0.08 us
  waiting for transfers between devices: 35.8 us -> 55 us
    gather x16 -> x0, local copies, waits for them, and re-layouts: 178 us -> none  [attend_entry(): return attend_query(entry[0], key_table[entry[1]], entry[2])]
    dot_general x36 -> x0, matrix products: 57.9 us -> none  [the longest x16 32 us: attend_query(): lax.dot_general(one_query, key_rows, (((1,), (1,)), ((), ())), preferred_...]
    pallas_call x0 -> x3, Pallas kernels: none -> 34.1 us  [the longest x1 18.9 us: on_device(): pl.pallas_call(functools.partial(attend_kernel, members, 4 if columns <=...]
    all_gather x2, waiting for transfers between devices: 26.7 us -> 54.3 us  [the longest x1 52 us: on_device(): table = lax.all_gather(latent_cache, 'ctx', axis=0, tiled=True)]
    scatter x5 -> x0, local copies, waits for them, and re-layouts: 27.1 us -> none  [the longest x1 8.64 us: on_device(): send_latent = jnp.zeros((members, capacity) + latent_pages.shape[1:], jnp...]
    all_gather x0 -> x1, blocking collectives: none -> 24 us  [on_device(): all_slots = lax.all_gather(row_slot, 'ctx', axis=1, tiled=True)]
    all_to_all x3 -> x0, starting transfers between devices: 19.5 us -> none  [the longest x1 7.48 us: on_device(): lax.all_to_all(send_slots, 'ctx', split_axis=0, concat_axis=0, tiled=True)]
    select_n x18 -> x0, other arithmetic: 14.3 us -> none  [the longest x16 13.7 us: attend_entry(): return attend_query(entry[0], key_table[entry[1]], entry[2])]
  transfers between devices with their start and end apart: 5 -> 2, of which waited for: 2 -> 2; matrix products, arithmetic and copies ran while one was open for 12% -> 5% of each run, Pallas kernels for 0% -> 11%
where the time goes in v1:
time: 137 us; the launch traced here: 136 us
  waiting for transfers between devices  55 us (40%)
  Pallas kernels  34.1 us (25%)
  blocking collectives  24 us (18%)
  between operations  14.1 us (10%)
  local copies, waits for them, and re-layouts  8.81 us (6%)
    all_gather x1, waiting for transfers between devices, on_device(): table = lax.all_gather(latent_cache, 'ctx', axis=0, tiled=True)  52 us
    all_gather x1, blocking collectives, on_device(): all_slots = lax.all_gather(row_slot, 'ctx', axis=1, tiled=True)  24 us
    pallas_call x1, Pallas kernels, on_device(): pl.pallas_call(functools.partial(attend_kernel, members, 4 if columns <=...  18.9 us
    pallas_call x1, Pallas kernels, on_device(): pl.pallas_call(functools.partial(prepare_kernel, members, local_rows), ou...  9.32 us
    unnamed x6, local copies, waits for them, and re-layouts  6.23 us
    pallas_call x1, Pallas kernels, on_device(): pl.pallas_call(functools.partial(index_kernel, index_heads), out_shape=ja...  5.91 us
  transfers between devices with their start and end apart: 2, of which 2 were waited for; matrix products, arithmetic and copies ran while one was open for 5% of the time, Pallas kernels for 11%

profile of v1, /device:TPU:1, one launch (start us, length us, event | category | flops | bytes accessed | tf_op | source)
XLA Modules:
  0.0 136.1 jit_solution(7702012403995850986)
XLA Ops:
  7.2 0.0 all-gather.3.cloned.1.call-start
  7.2 0.7 all-gather.3.cloned.1.call-update
  7.9 0.0 all-gather.5.cloned.1.call-start
  7.9 1.9 %copy.17 = bf16[256,576]{1,0:T(8,128)(2,1)} copy(bf16[256,576]{0,1:T(8,128)(2,1)} %param.13) | data formatting | bytes 589824 | tf_op args[4]
  9.8 0.0 copy-start.1
  9.8 0.0 copy-start
  9.8 0.0 all-gather.5.cloned.1.call-update
  9.8 4.4 %copy.18.query_ref = bf16[16,128,576]{2,1,0:T(8,128)(2,1)} copy(bf16[16,128,576]{1,2,0:T(8,128)(2,1)} %param.12) | data formatting | bytes 4718592 | tf_op args[3]
  14.2 0.0 copy-done.1
  14.2 0.1 iota_add_fusion
  14.3 0.1 add.26
  14.4 0.0 copy-done
  14.4 0.7 copy.16.place_ref
  15.1 24.0 %all_gather.10.slot_ref = s32[1,4096]{1,0:T(1,128)} all-gather(s32[1,256]{1,0:T(1,128)S(1)} %add.26), channel_id=1, replica_groups=mesh['groups'=2,'ctx'=16] {'ctx'}, dimensions={1}, use_global_device_ids=true | all-gather | bytes 17408 | tf_op jit(solution)/shard_map/all_gather | solution.py:186
  39.1 9.3 %prepare.1 = (bf16[16,64,256]{2,1,0:T(8,128)(2,1)}, f32[16,1280]{1,0:T(8,128)}) custom-call(s32[1]{0:T(128)} %bitcast.1.me_ref, s32[16,2048]{1,0:T(8,128)} %keys_ref.1, s32[16]{0:T(128)} %count_ref.1), custom_call_target="tpu_custom_call" | custom-call | flops 1000000000 | bytes 10000000 | tf_op jit(solution)/shard_map/prepare/pallas_call | solution.py:188
  48.4 2.3 %all-gather.3.cloned.1.call-done.keys_ref.index_ref = bf16[4096,128]{1,0:T(8,128)(2,1)} async-done(((bf16[256,128]{1,0:T(8,128)(2,1)}), bf16[4096,128]{1,0:T(8,128)(2,1)}) %all-gather.3.cloned.1.call-update) | async-done | bytes 1048592 | tf_op jit(solution)/shard_map/all_gather | solution.py:184
  50.7 5.9 %index_scores.1 = f32[16,4096]{1,0:T(8,128)} custom-call(bf16[16,8192]{1,0:T(8,128)(2,1)} %query_ref.2, f32[16,64]{1,0:T(8,128)} %weight_ref.1, bf16[4096,128]{1,0:T(8,128)(2,1)} %all-gather.3.cloned.1.call-done.keys_ref.index_ref, s32[16,1]{1,0:T(8,128)} %copy.16.place_ref), custom_call_target="tpu_custom_call" | custom-call | flops 1000000000 | bytes 20000000 | tf_op jit(solution)/shard_map/index_scores/pallas_call | solution.py:202
  56.7 52.0 %all-gather.5.cloned.1.call-done.table_ref = bf16[4096,576]{1,0:T(8,128)(2,1)} async-done(((bf16[256,576]{1,0:T(8,128)(2,1)}), bf16[4096,576]{1,0:T(8,128)(2,1)}) %all-gather.5.cloned.1.call-update) | async-done | bytes 4718608 | tf_op jit(solution)/shard_map/all_gather | solution.py:185
  108.6 18.9 %attend.1 = (bf16[16,128,512]{2,1,0:T(8,128)(2,1)}, bf16[256,576]{1,0:T(8,128)(2,1)}, bf16[256,128]{1,0:T(8,128)(2,1)}) custom-call(s32[1]{0:T(128)} %bitcast.1.me_ref, s32[1,4096]{1,0:T(1,128)} %all_gather.10.slot_ref, bf16[16,64,256]{2,1,0:T(8,128)(2,1)} %get-tuple-element.9.pick_ref, f32[16,1280]{1,0:T(8,128)} %get-tuple-element.10.bias_ref, ...), custom_call_target="tpu_custom_call" | custom-call | tf_op jit(solution)/shard_map/attend/pallas_call | solution.py:216
  127.5 1.8 %reshape.43 = bf16[64,4,576]{2,1,0:T(4,128)(2,1)} reshape(bf16[256,576]{1,0:T(8,128)(2,1)} %get-tuple-element.12) | data formatting | bytes 589824 | tf_op jit(solution)/shard_map/reshape | solution.py:235
  (1 shorter events, 0.0 us)
Async XLA Ops:
  7.2 43.6 %all-gather.3.cloned.1.call-start = ((), (), s32[]{:S(2)}) async-start(), calls=%async_computation | async-start | bytes 1114112 | tf_op jit(solution)/shard_map/all_gather | solution.py:184
  7.9 100.7 %all-gather.5.cloned.1.call-start = ((), (), s32[]{:S(2)}) async-start(), calls=%async_computation.1 | async-start | bytes 5570560 | tf_op jit(solution)/shard_map/all_gather | solution.py:185
  9.8 4.4 %copy-start.1 = (s32[64]{0:T(128)S(1)}, s32[64]{0:T(128)}, u32[]{:S(2)}) copy-start(s32[64]{0:T(128)} %param.17) | copy-start | bytes 772
  9.8 4.6 %copy-start = (s32[16]{0:T(128)S(1)}, s32[16]{0:T(128)}, u32[]{:S(2)}) copy-start(s32[16]{0:T(128)} %param.14) | copy-start | bytes 196
Sparse Core Ops, SparseCore 0:
  10.2 40.5 all-gather.2
  53.6 54.9 all-gather.4

commit v2 on v1

v2 whole, which is shorter than its diff:
```python
import functools
import math

import jax
import jax.numpy as jnp
from jax import lax
from jax.experimental import pallas as pl
from jax.experimental.pallas import tpu as pltpu
from jax.sharding import PartitionSpec as P

LAT = 512
PAGE = 4
FETCH = 64
LANES = 128
neg_fill = -1e30
score_scale = 192.0 ** (-0.5)
NT = (((1,), (1,)), ((), ()))


def exchange_kernel(
    members, heads, group,
    row_ref, index_ref, slot_ref, keys_ref, count_ref, query_ref, weight_ref, place_ref,
    index_out, chosen_out, bias_ref, latent_out, page_out,
    table, index_all, slot_all, marks, pick_ref, stacked, spread, latent_sum, page_sum,
    send_sem, recv_sem,
):
    me = lax.axis_index("ctx")
    core, side, depth = lax.rem(me, 2), lax.rem(me // 2, 2), members // 4
    far = me // 4
    row, local_rows = row_ref.shape
    queries, slots = keys_ref.shape
    per = local_rows // LANES
    blocks = members * per

    def at(z, y, c):
        return z * 4 + y * 2 + c

    above = at(lax.rem(far + 1, depth), side, core)
    below = at(lax.rem(far + depth - 1, depth), side, core)
    across = at(far, 1 - side, core)
    twin = at(far, side, 1 - core)
    has_above, has_below = far + 1 < depth, far > 0

    def copies(owner, target, way):
        return [
            pltpu.make_async_remote_copy(
                src_ref=ref.at[owner],
                dst_ref=ref.at[owner],
                send_sem=send_sem.at[way, kind, owner],
                recv_sem=recv_sem.at[kind, owner],
                device_id={"ctx": target},
                device_id_type=pl.DeviceIdType.MESH,
            )
            for kind, ref in enumerate((index_all, slot_all, table))
        ]

    def send(owner, target, way):
        for copy in copies(owner, target, way):
            copy.start()

    def arrived(owner):
        for copy in copies(owner, twin, 3):
            copy.wait_recv()

    table[me] = row_ref[...]
    index_all[me] = index_ref[...]
    slot_all[me] = slot_ref[...]

    barrier = pltpu.get_barrier_semaphore()

    def greet(target):
        pl.semaphore_signal(
            barrier, inc=1, device_id={"ctx": target}, device_id_type=pl.DeviceIdType.MESH
        )

    greet(across)
    greet(twin)
    pl.when(has_above)(lambda: greet(above))
    pl.when(has_below)(lambda: greet(below))
    pl.semaphore_wait(barrier, 2 + has_above.astype(jnp.int32) + has_below.astype(jnp.int32))

    send(me, across, 2)
    pl.when(has_above)(lambda: send(me, above, 0))
    pl.when(has_below)(lambda: send(me, below, 1))
    send(me, twin, 3)

    def mark(q, carry):
        keys = keys_ref[pl.ds(q, 1), :]
        live = lax.broadcasted_iota(jnp.int32, (1, slots), 1) < count_ref[q]
        keys = jnp.where(live, keys, -1)
        high = jnp.broadcast_to(keys >> 7, (blocks, slots))
        low = jnp.broadcast_to(keys & 127, (LANES, slots))
        in_block = (high == lax.broadcasted_iota(jnp.int32, (blocks, slots), 0)).astype(jnp.bfloat16)
        in_lane = (low == lax.broadcasted_iota(jnp.int32, (LANES, slots), 0)).astype(jnp.bfloat16)
        marks[:, pl.ds(q, 1), :] = lax.dot_general(
            in_block, in_lane, NT, preferred_element_type=jnp.float32
        ).reshape(blocks, 1, LANES)
        return carry

    def owner_marks(owner):
        return jnp.concatenate([marks[owner * per + k] for k in range(per)], axis=1)

    early = queries * 3 // 4

    def prepare():
        lax.fori_loop(early, queries, mark, 0)
        before = (
            lax.broadcasted_iota(jnp.int32, (local_rows, local_rows), 0)
            < lax.broadcasted_iota(jnp.int32, (local_rows, local_rows), 1)
        ).astype(jnp.bfloat16)
        place = lax.broadcasted_iota(jnp.int32, (2 * FETCH, local_rows), 0)

        def compact(owner, half):
            own = owner_marks(owner)
            used = jnp.max(own, axis=0, keepdims=True)
            used = used * jnp.where(me == owner, 0.0, 1.0)
            rank = jnp.dot(
                jnp.broadcast_to(used, (16, local_rows)).astype(jnp.bfloat16),
                before,
                preferred_element_type=jnp.float32,
            )[:1]
            rank = jnp.where(used > 0.5, rank, -1.0)
            rows = (place - half * FETCH).astype(jnp.float32)
            inside = jnp.broadcast_to(rank, (2 * FETCH, local_rows))
            pick = ((inside == rows) & (inside > -0.5)).astype(jnp.bfloat16)
            pick_ref[owner] = pick
            return lax.dot_general(
                own.astype(jnp.bfloat16), pick, NT, preferred_element_type=jnp.float32
            )

        def pair_bias(pair, carry):
            named = compact(2 * pair, 0) + compact(2 * pair + 1, 1)
            bias_ref[:, pl.ds(pl.multiple_of(pair * LANES, LANES), LANES)] = jnp.where(
                named > 0.5, 0.0, neg_fill
            )
            return carry

        lax.fori_loop(0, members // 2, pair_bias, 0)
        bias_ref[:, members * FETCH :] = jnp.where(owner_marks(me) > 0.5, 0.0, neg_fill)
        chosen_out[:, members * FETCH :] = row_ref[...]

    width = index_ref.shape[1]
    for h in range(heads):
        stacked[h * queries : (h + 1) * queries, :] = query_ref[:, h * width : (h + 1) * width]
        spread[h * queries : (h + 1) * queries, :] = jnp.broadcast_to(
            weight_ref[:, h : h + 1], (queries, LANES)
        )
    latent_sum[...] = jnp.zeros_like(latent_sum)
    page_sum[...] = jnp.zeros_like(page_sum)
    lax.fori_loop(0, early, mark, 0)

    def use(z, y):
        first = at(z, y, 0)
        named = jnp.zeros((row, 2 * FETCH), jnp.float32)
        for half in range(2):
            owner = first + half
            keys = index_all[owner]
            rows = table[owner]
            total = jnp.zeros((queries, local_rows), jnp.float32)
            for g in range(heads // group):
                part = slice(g * group * queries, (g + 1) * group * queries)
                raw = lax.dot_general(
                    stacked[part, :], keys, NT, preferred_element_type=jnp.float32
                )
                raw = jnp.maximum(raw, 0.0)
                for k in range(group):
                    weight = spread[(g * group + k) * queries : (g * group + k + 1) * queries, :]
                    total = total + raw[k * queries : (k + 1) * queries] * jnp.concatenate(
                        [weight] * per, axis=1
                    )
            start = pl.multiple_of(owner * local_rows, local_rows)
            columns = start + lax.broadcasted_iota(jnp.int32, (queries, local_rows), 1)
            places = jnp.broadcast_to(place_ref[...], (queries, local_rows))
            index_out[:, pl.ds(start, local_rows)] = jnp.where(columns <= places, total, 0.0)
            named = named + lax.dot_general(
                rows, pick_ref[owner], NT, preferred_element_type=jnp.float32
            )
            goal = me * local_rows + lax.broadcasted_iota(jnp.int32, (local_rows, local_rows), 0)
            moved = (
                jnp.broadcast_to(slot_all[owner], (local_rows, local_rows)) == goal
            ).astype(jnp.bfloat16)
            latent_sum[...] += lax.dot_general(moved, rows, NT, preferred_element_type=jnp.float32)
            page_sum[...] += jnp.dot(moved, keys, preferred_element_type=jnp.float32)
        chosen_out[:, pl.ds(pl.multiple_of(first * FETCH, 2 * FETCH), 2 * FETCH)] = named.astype(
            jnp.bfloat16
        )

    def hop(k, carry):
        @pl.when(far - k >= 0)
        def _():
            owner = at(far - k, side, core)
            arrived(owner)
            pl.when(has_above)(lambda: send(owner, above, 0))
            send(owner, across, 2)
            send(owner, twin, 3)

        @pl.when(far + k < depth)
        def _():
            owner = at(far + k, side, core)
            arrived(owner)
            pl.when(has_below)(lambda: send(owner, below, 1))
            send(owner, across, 2)
            send(owner, twin, 3)

        def from_across(z):
            owner = at(z, 1 - side, core)
            arrived(owner)
            send(owner, twin, 3)

        last = k - 1
        behind = far - last >= 0
        ahead = (far + last < depth) & (last > 0)
        pl.when(behind)(lambda: from_across(far - last))
        pl.when(ahead)(lambda: from_across(far + last))
        pl.when(last == 0)(prepare)

        def finish(z, y):
            arrived(at(z, y, 1 - core))
            use(z, y)

        def finish_all(i, carry):
            z = far + (2 * (i // 2) - 1) * last
            y = lax.rem(side + lax.rem(i, 2), 2)
            pl.when((z >= 0) & (z < depth) & ((last > 0) | (i < 2)))(lambda: finish(z, y))
            return carry

        lax.fori_loop(0, 4, finish_all, 0)
        return carry

    lax.fori_loop(1, depth + 1, hop, 0)
    latent_out[...] = latent_sum[...].astype(jnp.bfloat16)
    page_out[...] = page_sum[...].astype(jnp.bfloat16)

    def sent(owner, target, way):
        for copy in copies(owner, target, way):
            copy.wait_send()

    def drain(z, carry):
        owner = at(z, side, core)
        pl.when(has_above & (z <= far))(lambda: sent(owner, above, 0))
        pl.when(has_below & (z >= far))(lambda: sent(owner, below, 1))
        sent(owner, across, 2)
        sent(owner, twin, 3)
        sent(at(z, 1 - side, core), twin, 3)
        return carry

    lax.fori_loop(0, depth, drain, 0)


def attend_kernel(bias_ref, query_ref, chosen_ref, out_ref):
    group, row, heads = query_ref.shape
    factor = score_scale * math.log2(math.e)
    first = pl.program_id(0) * group
    query = jnp.concatenate([query_ref[k].T for k in range(group)], axis=0)
    scores = jnp.dot(query, chosen_ref[...], preferred_element_type=jnp.float32)
    shares, sums = [], []
    for k in range(group):
        part = scores[k * heads : (k + 1) * heads] + bias_ref[pl.ds(first + k, 1), :]
        highest = jnp.max(part, axis=1, keepdims=True)
        lifted = jnp.exp2((part - highest) * factor)
        sums.append(jnp.sum(lifted, axis=1, keepdims=True))
        shares.append(lifted.astype(jnp.bfloat16))
    total = lax.dot_general(
        jnp.concatenate(shares, axis=0), chosen_ref[:LAT, :], NT, preferred_element_type=jnp.float32
    )
    total = total / jnp.concatenate(sums, axis=0)
    out_ref[...] = total.astype(jnp.bfloat16).reshape(group, heads, LAT)


VMEM = pl.BlockSpec(memory_space=pltpu.VMEM)
SMEM = pl.BlockSpec(memory_space=pltpu.SMEM)


def on_device(
    index_query, index_weight, index_keys, attn_query, latent_cache, positions, sel_keys,
    sel_count, page_slot,
):
    members = lax.axis_size("ctx")
    local_rows, row = latent_cache.shape
    queries, index_heads = index_weight.shape
    head_width = index_keys.shape[1]
    attn_heads = attn_query.shape[1]
    total_rows = members * local_rows
    columns = members * FETCH + local_rows
    row_slot = (page_slot[:, None] * PAGE + jnp.arange(PAGE, dtype=jnp.int32)[None, :]).reshape(1, -1)

    index_scores, chosen, bias, decode_latent, decode_index = pl.pallas_call(
        functools.partial(exchange_kernel, members, index_heads, 16),
        out_shape=(
            jax.ShapeDtypeStruct((queries, total_rows), jnp.float32),
            jax.ShapeDtypeStruct((row, columns), jnp.bfloat16),
            jax.ShapeDtypeStruct((queries, columns), jnp.float32),
            jax.ShapeDtypeStruct((local_rows, row), jnp.bfloat16),
            jax.ShapeDtypeStruct((local_rows, head_width), jnp.bfloat16),
        ),
        in_specs=[VMEM] * 4 + [SMEM] + [VMEM] * 3,
        out_specs=(VMEM,) * 5,
        scratch_shapes=[
            pltpu.VMEM((members, row, local_rows), jnp.bfloat16),
            pltpu.VMEM((members, local_rows, head_width), jnp.bfloat16),
            pltpu.VMEM((members, 1, local_rows), jnp.int32),
            pltpu.VMEM((total_rows // LANES, queries, LANES), jnp.float32),
            pltpu.VMEM((members, 2 * FETCH, local_rows), jnp.bfloat16),
            pltpu.VMEM((index_heads * queries, head_width), jnp.bfloat16),
            pltpu.VMEM((index_heads * queries, LANES), jnp.float32),
            pltpu.VMEM((local_rows, row), jnp.float32),
            pltpu.VMEM((local_rows, head_width), jnp.float32),
            pltpu.SemaphoreType.DMA((4, 3, members)),
            pltpu.SemaphoreType.DMA((3, members)),
        ],
        compiler_params=pltpu.CompilerParams(
            collective_id=0, has_side_effects=True, vmem_limit_bytes=60 * 2**20
        ),
        name="exchange",
    )(
        latent_cache.T, index_keys, row_slot, sel_keys, sel_count, index_query, index_weight,
        positions[:, None],
    )

    group = 4 if columns <= 2048 else 2
    attn_latent = pl.pallas_call(
        attend_kernel,
        grid=(queries // group,),
        out_shape=jax.ShapeDtypeStruct((queries, attn_heads, LAT), jnp.bfloat16),
        in_specs=[
            pl.BlockSpec((queries, columns), lambda g: (0, 0)),
            pl.BlockSpec((group, row, attn_heads), lambda g: (g, 0, 0)),
            pl.BlockSpec((row, columns), lambda g: (0, 0)),
        ],
        out_specs=pl.BlockSpec((group, attn_heads, LAT), lambda g: (g, 0, 0)),
        compiler_params=pltpu.CompilerParams(vmem_limit_bytes=60 * 2**20),
        name="attend",
    )(bias, jnp.swapaxes(attn_query, 1, 2), chosen)
    return (
        index_scores,
        attn_latent,
        decode_latent.reshape(local_rows // PAGE, PAGE, row),
        decode_index.reshape(local_rows // PAGE, PAGE, head_width),
    )


def solution(mesh):
    rows = P(("groups", "ctx"), None)
    deep = P(("groups", "ctx"), None, None)
    flat = P(("groups", "ctx"))
    return jax.shard_map(
        on_device,
        mesh=mesh,
        in_specs=(rows, rows, rows, deep, rows, flat, rows, flat, flat),
        out_specs=(rows, deep, deep, deep),
        check_vma=False,
    )
```

time: 137 us -> 64.4 us (0.47)
  waiting for transfers between devices: 55 us -> 0 us
  blocking collectives: 24 us -> 0 us
  Pallas kernels: 34.1 us -> 57.7 us
  between operations: 14.1 us -> 0.64 us
  local copies, waits for them, and re-layouts: 8.81 us -> 5.13 us
    all_gather x2 -> x0, waiting for transfers between devices: 54.3 us -> none  [the longest x1 52 us: on_device(): table = lax.all_gather(latent_cache, 'ctx', axis=0, tiled=True)]
    all_gather x1 -> x0, blocking collectives: 24 us -> none  [on_device(): all_slots = lax.all_gather(row_slot, 'ctx', axis=1, tiled=True)]
    pallas_call x3 -> x2, Pallas kernels: 34.1 us -> 57.7 us  [the longest x1 46.2 us: on_device(): pl.pallas_call(functools.partial(exchange_kernel, members, index_heads, 1...]
    unnamed x6, local copies, waits for them, and re-layouts: 6.23 us -> 1.34 us
  transfers between devices with their start and end apart: 2 -> 0, of which waited for: 2 -> 0; matrix products, arithmetic and copies ran while one was open for 5% -> 0% of each run, Pallas kernels for 11% -> 0%
where the time goes in v2:
time: 64.4 us; the launch traced here: 64.2 us
  Pallas kernels  57.7 us (90%)
  local copies, waits for them, and re-layouts  5.13 us (8%)
  other arithmetic  0.73 us (1%)
    pallas_call x1, Pallas kernels, on_device(): pl.pallas_call(functools.partial(exchange_kernel, members, index_heads, 1...  46.2 us
    pallas_call x1, Pallas kernels, on_device(): pl.pallas_call(attend_kernel, grid=(queries // group,), out_shape=jax.Sha...  11.5 us
    reshape x1, local copies, waits for them, and re-layouts, on_device(): decode_latent.reshape(local_rows // PAGE, PAGE, row)  1.79 us
    unnamed x6, local copies, waits for them, and re-layouts  1.34 us
    broadcast_in_dim x1, local copies, waits for them, and re-layouts, on_device(): positions[:, None]  1.33 us

profile of v2, /device:TPU:1, one launch (start us, length us, event | category | flops | bytes accessed | tf_op | source)
XLA Modules:
  0.0 64.2 jit_solution(15631152750188777362)
XLA Ops:
  0.6 0.7 %broadcast_multiply_fusion = s32[64]{0:T(128)S(1)} fusion(s32[64]{0:T(128)} %param.17), kind=kLoop, calls=%fused_computation.1 | loop fusion | flops 64 | bytes 512 | tf_op jit(solution)/shard_map/mul | solution.py:285
  1.3 1.3 %copy.14.place_ref = s32[16,1]{1,0:T(8,128)} copy(s32[16,1]{0,1:T(1,128)} %bitcast.7) | data formatting | bytes 128 | tf_op jit(solution)/shard_map/broadcast_in_dim | solution.py:317
  2.6 0.1 iota_add_fusion
  2.7 0.7 %add.26.slot_ref = s32[1,256]{1,0:T(1,128)} reshape(s32[64,4]{1,0:T(8,128)S(1)} %iota_add_fusion) | data formatting | bytes 2048 | tf_op jit(solution)/shard_map/add | solution.py:285
  3.4 46.2 %exchange.1 = (f32[16,4096]{1,0:T(8,128)}, bf16[576,1280]{1,0:T(8,128)(2,1)}, f32[16,1280]{1,0:T(8,128)}, bf16[256,576]{1,0:T(8,128)(2,1)}, bf16[256,128]{1,0:T(8,128)(2,1)}) custom-call(bf16[576,256]{1,0:T(8,128)(2,1)} %bitcast.5, bf16[256,128]{1,0:T(8,128)(2,1)} %index_ref.1, s32[1,256]{1,0:T(1,128)} %add.26.slot_ref, s32[16,2048]{1,0:T(8,128)} %keys_ref.1, ...), custom_call_target="tpu_custom_call" | custom-call | tf_op jit(solution)/shard_map/exchange/pallas_call | solution.py:287
  49.6 1.8 %reshape.39 = bf16[64,4,576]{2,1,0:T(4,128)(2,1)} reshape(bf16[256,576]{1,0:T(8,128)(2,1)} %get-tuple-element.12) | data formatting | bytes 589824 | tf_op jit(solution)/shard_map/reshape | solution.py:337
  51.4 0.0 copy-start
  51.4 0.0 copy-start.1
  51.4 11.5 %attend.1 = bf16[16,128,512]{2,1,0:T(8,128)(2,1)} custom-call(f32[16,1280]{1,0:T(8,128)} %get-tuple-element.10.bias_ref, bf16[16,576,128]{2,1,0:T(8,128)(2,1)} %bitcast.4, bf16[576,1280]{1,0:T(8,128)(2,1)} %get-tuple-element.11.chosen_ref), custom_call_target="tpu_custom_call" | custom-call | tf_op jit(solution)/shard_map/attend/pallas_call | solution.py:321
  62.9 0.0 copy-done
  62.9 0.7 %copy.17 = f32[16,4096]{1,0:T(8,128)} copy(f32[16,4096]{1,0:T(8,128)S(1)} %copy-done) | data formatting | bytes 524288
  63.6 0.0 copy-done.1
  63.6 0.6 copy.18
Async XLA Ops:
  51.4 11.5 %copy-start = (f32[16,4096]{1,0:T(8,128)S(1)}, f32[16,4096]{1,0:T(8,128)}, u32[]{:S(2)}) copy-start(f32[16,4096]{1,0:T(8,128)} %get-tuple-element.18) | copy-start | bytes 786436
  51.4 12.2 %copy-start.1 = (bf16[256,128]{1,0:T(8,128)(2,1)S(1)}, bf16[256,128]{1,0:T(8,128)(2,1)}, u32[]{:S(2)}) copy-start(bf16[256,128]{1,0:T(8,128)(2,1)} %get-tuple-element.13) | copy-start | bytes 196612

commit v3 on v2

--- a/solution.py
+++ b/solution.py
@@ -20,8 +20,8 @@
 def exchange_kernel(
     members, heads, group,
     row_ref, index_ref, slot_ref, keys_ref, count_ref, query_ref, weight_ref, place_ref,
-    index_out, chosen_out, bias_ref, latent_out, page_out,
-    table, index_all, slot_all, marks, pick_ref, stacked, spread, latent_sum, page_sum,
+    index_out, chosen_out, bias_ref, latent_sum, page_sum,
+    table, index_all, slot_all, marks, pick_ref, stacked, spread, places_all,
     send_sem, recv_sem,
 ):
     me = lax.axis_index("ctx")
@@ -64,7 +64,18 @@
 
     table[me] = row_ref[...]
     index_all[me] = index_ref[...]
-    slot_all[me] = slot_ref[...]
+    pages = slot_ref.shape[1]
+    fine = lax.broadcasted_iota(jnp.int32, (pages, local_rows), 1)
+    spread_pages = (
+        (fine // PAGE) == lax.broadcasted_iota(jnp.int32, (pages, local_rows), 0)
+    ).astype(jnp.bfloat16)
+
+    def widen(values):
+        values = jnp.broadcast_to(values.astype(jnp.float32), (16, pages)).astype(jnp.bfloat16)
+        return jnp.dot(values, spread_pages, preferred_element_type=jnp.float32)[:1]
+
+    slot = widen(slot_ref[...] >> 6) * 64.0 + widen(slot_ref[...] & 63)
+    slot_all[me] = slot.astype(jnp.int32) * PAGE + fine[:1] % PAGE
 
     barrier = pltpu.get_barrier_semaphore()
 
@@ -145,6 +156,11 @@
         spread[h * queries : (h + 1) * queries, :] = jnp.broadcast_to(
             weight_ref[:, h : h + 1], (queries, LANES)
         )
+    seat = lax.broadcasted_iota(jnp.int32, (queries, LANES), 0)
+    places_here = jnp.zeros((queries, LANES), jnp.int32)
+    for q in range(queries):
+        places_here = jnp.where(seat == q, place_ref[q], places_here)
+    places_all[...] = places_here
     latent_sum[...] = jnp.zeros_like(latent_sum)
     page_sum[...] = jnp.zeros_like(page_sum)
     lax.fori_loop(0, early, mark, 0)
@@ -170,7 +186,7 @@
                     )
             start = pl.multiple_of(owner * local_rows, local_rows)
             columns = start + lax.broadcasted_iota(jnp.int32, (queries, local_rows), 1)
-            places = jnp.broadcast_to(place_ref[...], (queries, local_rows))
+            places = jnp.concatenate([places_all[...]] * per, axis=1)
             index_out[:, pl.ds(start, local_rows)] = jnp.where(columns <= places, total, 0.0)
             named = named + lax.dot_general(
                 rows, pick_ref[owner], NT, preferred_element_type=jnp.float32
@@ -228,8 +244,6 @@
         return carry
 
     lax.fori_loop(1, depth + 1, hop, 0)
-    latent_out[...] = latent_sum[...].astype(jnp.bfloat16)
-    page_out[...] = page_sum[...].astype(jnp.bfloat16)
 
     def sent(owner, target, way):
         for copy in copies(owner, target, way):
@@ -247,8 +261,15 @@
     lax.fori_loop(0, depth, drain, 0)
 
 
-def attend_kernel(bias_ref, query_ref, chosen_ref, out_ref):
+def attend_kernel(
+    bias_ref, query_ref, chosen_ref, scores_ref, latent_ref, page_ref,
+    out_ref, scores_out, latent_out, page_out,
+):
     group, row, heads = query_ref.shape
+    scores_out[...] = scores_ref[...]
+    for page in range(latent_out.shape[0]):
+        latent_out[page] = latent_ref[page * PAGE : (page + 1) * PAGE, :].astype(jnp.bfloat16)
+        page_out[page] = page_ref[page * PAGE : (page + 1) * PAGE, :].astype(jnp.bfloat16)
     factor = score_scale * math.log2(math.e)
     first = pl.program_id(0) * group
     query = jnp.concatenate([query_ref[k].T for k in range(group)], axis=0)
@@ -282,18 +303,17 @@
     attn_heads = attn_query.shape[1]
     total_rows = members * local_rows
     columns = members * FETCH + local_rows
-    row_slot = (page_slot[:, None] * PAGE + jnp.arange(PAGE, dtype=jnp.int32)[None, :]).reshape(1, -1)
-
-    index_scores, chosen, bias, decode_latent, decode_index = pl.pallas_call(
+
+    scores, chosen, bias, decode_latent, decode_index = pl.pallas_call(
         functools.partial(exchange_kernel, members, index_heads, 16),
         out_shape=(
             jax.ShapeDtypeStruct((queries, total_rows), jnp.float32),
             jax.ShapeDtypeStruct((row, columns), jnp.bfloat16),
             jax.ShapeDtypeStruct((queries, columns), jnp.float32),
-            jax.ShapeDtypeStruct((local_rows, row), jnp.bfloat16),
-            jax.ShapeDtypeStruct((local_rows, head_width), jnp.bfloat16),
+            jax.ShapeDtypeStruct((local_rows, row), jnp.float32),
+            jax.ShapeDtypeStruct((local_rows, head_width), jnp.float32),
         ),
-        in_specs=[VMEM] * 4 + [SMEM] + [VMEM] * 3,
+        in_specs=[VMEM] * 4 + [SMEM] + [VMEM] * 2 + [SMEM],
         out_specs=(VMEM,) * 5,
         scratch_shapes=[
             pltpu.VMEM((members, row, local_rows), jnp.bfloat16),
@@ -303,8 +323,7 @@
             pltpu.VMEM((members, 2 * FETCH, local_rows), jnp.bfloat16),
             pltpu.VMEM((index_heads * queries, head_width), jnp.bfloat16),
             pltpu.VMEM((index_heads * queries, LANES), jnp.float32),
-            pltpu.VMEM((local_rows, row), jnp.float32),
-            pltpu.VMEM((local_rows, head_width), jnp.float32),
+            pltpu.VMEM((queries, LANES), jnp.int32),
             pltpu.SemaphoreType.DMA((4, 3, members)),
             pltpu.SemaphoreType.DMA((3, members)),
         ],
@@ -313,30 +332,40 @@
         ),
         name="exchange",
     )(
-        latent_cache.T, index_keys, row_slot, sel_keys, sel_count, index_query, index_weight,
-        positions[:, None],
+        latent_cache.T, index_keys, page_slot.reshape(1, -1), sel_keys, sel_count, index_query,
+        index_weight, positions,
     )
 
     group = 4 if columns <= 2048 else 2
-    attn_latent = pl.pallas_call(
+    steps = queries // group
+    pages = local_rows // PAGE
+    attn_latent, index_scores, decode_latent, decode_index = pl.pallas_call(
         attend_kernel,
-        grid=(queries // group,),
-        out_shape=jax.ShapeDtypeStruct((queries, attn_heads, LAT), jnp.bfloat16),
+        grid=(steps,),
+        out_shape=(
+            jax.ShapeDtypeStruct((queries, attn_heads, LAT), jnp.bfloat16),
+            jax.ShapeDtypeStruct((queries, total_rows), jnp.float32),
+            jax.ShapeDtypeStruct((pages, PAGE, row), jnp.bfloat16),
+            jax.ShapeDtypeStruct((pages, PAGE, head_width), jnp.bfloat16),
+        ),
         in_specs=[
             pl.BlockSpec((queries, columns), lambda g: (0, 0)),
             pl.BlockSpec((group, row, attn_heads), lambda g: (g, 0, 0)),
             pl.BlockSpec((row, columns), lambda g: (0, 0)),
+            pl.BlockSpec((queries, total_rows // steps), lambda g: (0, g)),
+            pl.BlockSpec((local_rows // steps, row), lambda g: (g, 0)),
+            pl.BlockSpec((local_rows // steps, head_width), lambda g: (g, 0)),
         ],
-        out_specs=pl.BlockSpec((group, attn_heads, LAT), lambda g: (g, 0, 0)),
+        out_specs=(
+            pl.BlockSpec((group, attn_heads, LAT), lambda g: (g, 0, 0)),
+            pl.BlockSpec((queries, total_rows // steps), lambda g: (0, g)),
+            pl.BlockSpec((pages // steps, PAGE, row), lambda g: (g, 0, 0)),
+            pl.BlockSpec((pages // steps, PAGE, head_width), lambda g: (g, 0, 0)),
+        ),
         compiler_params=pltpu.CompilerParams(vmem_limit_bytes=60 * 2**20),
         name="attend",
-    )(bias, jnp.swapaxes(attn_query, 1, 2), chosen)
-    return (
-        index_scores,
-        attn_latent,
-        decode_latent.reshape(local_rows // PAGE, PAGE, row),
-        decode_index.reshape(local_rows // PAGE, PAGE, head_width),
-    )
+    )(bias, jnp.swapaxes(attn_query, 1, 2), chosen, scores, decode_latent, decode_index)
+    return index_scores, attn_latent, decode_latent, decode_index
 
 
 def solution(mesh):

time: 64.4 us -> 58.8 us (0.913)
  local copies, waits for them, and re-layouts: 5.13 us -> 0 us
  other arithmetic: 0.73 us -> 0 us
    reshape x1 -> x0, local copies, waits for them, and re-layouts: 1.79 us -> none  [on_device(): decode_latent.reshape(local_rows // PAGE, PAGE, row)]
    unnamed x6 -> x0, local copies, waits for them, and re-layouts: 1.34 us -> none
    broadcast_in_dim x1 -> x0, local copies, waits for them, and re-layouts: 1.33 us -> none  [on_device(): positions[:, None]]
    add x1 -> x0, local copies, waits for them, and re-layouts: 0.68 us -> none  [on_device(): page_slot[:, None] * PAGE + jnp.arange(PAGE, dtype=jnp.int32)[None, :]]
    mul x1 -> x0, other arithmetic: 0.66 us -> none  [on_device(): page_slot[:, None] * PAGE + jnp.arange(PAGE, dtype=jnp.int32)[None, :]]
where the time goes in v3:
time: 58.8 us; the launch traced here: 58.7 us
  Pallas kernels  58 us (99%)
  between operations  0.64 us (1%)
    pallas_call x1, Pallas kernels, on_device(): pl.pallas_call(functools.partial(exchange_kernel, members, index_heads, 1...  46.4 us
    pallas_call x1, Pallas kernels, on_device(): pl.pallas_call(attend_kernel, grid=(steps,), out_shape=(jax.ShapeDtypeStr...  11.7 us

profile of v3, /device:TPU:1, one launch (start us, length us, event | category | flops | bytes accessed | tf_op | source)
XLA Modules:
  0.0 58.7 jit_solution(16590253342534039400)
XLA Ops:
  0.6 46.4 %exchange.1 = (f32[16,4096]{1,0:T(8,128)}, bf16[576,1280]{1,0:T(8,128)(2,1)}, f32[16,1280]{1,0:T(8,128)}, f32[256,576]{1,0:T(8,128)}, f32[256,128]{1,0:T(8,128)}) custom-call(bf16[576,256]{1,0:T(8,128)(2,1)} %bitcast.4, bf16[256,128]{1,0:T(8,128)(2,1)} %index_ref.1, s32[1,64]{1,0:T(1,128)} %bitcast.5, s32[16,2048]{1,0:T(8,128)} %keys_ref.1, s32[16]{0:T(128)} %count_ref.1, ...), custom_call_target="tpu_custom_call" | custom-call | tf_op jit(solution)/shard_map/exchange/pallas_call | solution.py:307
  47.0 11.7 %attend.1 = (bf16[16,128,512]{2,1,0:T(8,128)(2,1)}, f32[16,4096]{1,0:T(8,128)}, bf16[64,4,576]{2,1,0:T(4,128)(2,1)}, bf16[64,4,128]{2,1,0:T(4,128)(2,1)}) custom-call(f32[16,1280]{1,0:T(8,128)} %get-tuple-element.13.bias_ref, bf16[16,576,128]{2,1,0:T(8,128)(2,1)} %bitcast.3, bf16[576,1280]{1,0:T(8,128)(2,1)} %get-tuple-element.14.chosen_ref, ...), custom_call_target="tpu_custom_call" | custom-call | tf_op jit(solution)/shard_map/attend/pallas_call | solution.py:342

commit v4 on v3

--- a/solution.py
+++ b/solution.py
@@ -40,6 +40,9 @@
     across = at(far, 1 - side, core)
     twin = at(far, side, 1 - core)
     has_above, has_below = far + 1 < depth, far > 0
+
+    def early_cross(z):
+        return (core == 0) & ((z == 0) | (z == depth - 1))
 
     def copies(owner, target, way):
         return [
@@ -207,7 +210,7 @@
             owner = at(far - k, side, core)
             arrived(owner)
             pl.when(has_above)(lambda: send(owner, above, 0))
-            send(owner, across, 2)
+            pl.when(jnp.logical_not(early_cross(far - k)))(lambda: send(owner, across, 2))
             send(owner, twin, 3)
 
         @pl.when(far + k < depth)
@@ -215,12 +218,14 @@
             owner = at(far + k, side, core)
             arrived(owner)
             pl.when(has_below)(lambda: send(owner, below, 1))
-            send(owner, across, 2)
+            pl.when(jnp.logical_not(early_cross(far + k)))(lambda: send(owner, across, 2))
             send(owner, twin, 3)
 
         def from_across(z):
             owner = at(z, 1 - side, core)
             arrived(owner)
+            pl.when(early_cross(z) & has_above & (z <= far))(lambda: send(owner, above, 0))
+            pl.when(early_cross(z) & has_below & (z >= far))(lambda: send(owner, below, 1))
             send(owner, twin, 3)
 
         last = k - 1
@@ -253,9 +258,12 @@
         owner = at(z, side, core)
         pl.when(has_above & (z <= far))(lambda: sent(owner, above, 0))
         pl.when(has_below & (z >= far))(lambda: sent(owner, below, 1))
-        sent(owner, across, 2)
+        pl.when((z == far) | jnp.logical_not(early_cross(z)))(lambda: sent(owner, across, 2))
         sent(owner, twin, 3)
-        sent(at(z, 1 - side, core), twin, 3)
+        other = at(z, 1 - side, core)
+        pl.when(early_cross(z) & has_above & (z <= far))(lambda: sent(other, above, 0))
+        pl.when(early_cross(z) & has_below & (z >= far))(lambda: sent(other, below, 1))
+        sent(other, twin, 3)
         return carry
 
     lax.fori_loop(0, depth, drain, 0)

time: 58.8 us -> 56.2 us (0.956)
  Pallas kernels: 58 us -> 55.4 us
    pallas_call x1, Pallas kernels: 46.4 us -> 43.7 us  [on_device(): pl.pallas_call(functools.partial(exchange_kernel, members, index_heads, 1...]
where the time goes in v4:
time: 56.2 us; the launch traced here: 56 us
  Pallas kernels  55.4 us (99%)
  between operations  0.64 us (1%)
    pallas_call x1, Pallas kernels, on_device(): pl.pallas_call(functools.partial(exchange_kernel, members, index_heads, 1...  43.7 us
    pallas_call x1, Pallas kernels, on_device(): pl.pallas_call(attend_kernel, grid=(steps,), out_shape=(jax.ShapeDtypeStr...  11.7 us

profile of v4, /device:TPU:1, one launch (start us, length us, event | category | flops | bytes accessed | tf_op | source)
XLA Modules:
  0.0 56.0 jit_solution(11148806203350229204)
XLA Ops:
  0.6 43.7 %exchange.1 = (f32[16,4096]{1,0:T(8,128)}, bf16[576,1280]{1,0:T(8,128)(2,1)}, f32[16,1280]{1,0:T(8,128)}, f32[256,576]{1,0:T(8,128)}, f32[256,128]{1,0:T(8,128)}) custom-call(bf16[576,256]{1,0:T(8,128)(2,1)} %bitcast.4, bf16[256,128]{1,0:T(8,128)(2,1)} %index_ref.1, s32[1,64]{1,0:T(1,128)} %bitcast.5, s32[16,2048]{1,0:T(8,128)} %keys_ref.1, s32[16]{0:T(128)} %count_ref.1, ...), custom_call_target="tpu_custom_call" | custom-call | tf_op jit(solution)/shard_map/exchange/pallas_call | solution.py:315
  44.4 11.7 %attend.1 = (bf16[16,128,512]{2,1,0:T(8,128)(2,1)}, f32[16,4096]{1,0:T(8,128)}, bf16[64,4,576]{2,1,0:T(4,128)(2,1)}, bf16[64,4,128]{2,1,0:T(4,128)(2,1)}) custom-call(f32[16,1280]{1,0:T(8,128)} %get-tuple-element.13.bias_ref, bf16[16,576,128]{2,1,0:T(8,128)(2,1)} %bitcast.3, bf16[576,1280]{1,0:T(8,128)(2,1)} %get-tuple-element.14.chosen_ref, ...), custom_call_target="tpu_custom_call" | custom-call | tf_op jit(solution)/shard_map/attend/pallas_call | solution.py:350

commit v5 on v4

--- a/solution.py
+++ b/solution.py
@@ -44,18 +44,25 @@
     def early_cross(z):
         return (core == 0) & ((z == 0) | (z == depth - 1))
 
+    half = row // 2
+
+    def piece(kind, owner):
+        if kind < 2:
+            return (index_all, slot_all)[kind].at[owner]
+        return table.at[owner, pl.ds((kind - 2) * half, half), :]
+
+    def copy_of(kind, owner, target, way):
+        return pltpu.make_async_remote_copy(
+            src_ref=piece(kind, owner),
+            dst_ref=piece(kind, owner),
+            send_sem=send_sem.at[way, kind, owner],
+            recv_sem=recv_sem.at[kind, owner],
+            device_id={"ctx": target},
+            device_id_type=pl.DeviceIdType.MESH,
+        )
+
     def copies(owner, target, way):
-        return [
-            pltpu.make_async_remote_copy(
-                src_ref=ref.at[owner],
-                dst_ref=ref.at[owner],
-                send_sem=send_sem.at[way, kind, owner],
-                recv_sem=recv_sem.at[kind, owner],
-                device_id={"ctx": target},
-                device_id_type=pl.DeviceIdType.MESH,
-            )
-            for kind, ref in enumerate((index_all, slot_all, table))
-        ]
+        return [copy_of(kind, owner, target, way) for kind in range(4)]
 
     def send(owner, target, way):
         for copy in copies(owner, target, way):
@@ -64,6 +71,16 @@
     def arrived(owner):
         for copy in copies(owner, twin, 3):
             copy.wait_recv()
+
+    def relay(owner, routes):
+        for kind in range(4):
+            copy_of(kind, owner, twin, 3).wait_recv()
+            for condition, target, way in routes:
+                @pl.when(condition)
+                def _():
+                    copy_of(kind, owner, target, way).start()
+
+            copy_of(kind, owner, twin, 3).start()
 
     table[me] = row_ref[...]
     index_all[me] = index_ref[...]
@@ -208,25 +225,28 @@
         @pl.when(far - k >= 0)
         def _():
             owner = at(far - k, side, core)
-            arrived(owner)
-            pl.when(has_above)(lambda: send(owner, above, 0))
-            pl.when(jnp.logical_not(early_cross(far - k)))(lambda: send(owner, across, 2))
-            send(owner, twin, 3)
+            relay(
+                owner,
+                ((has_above, above, 0), (jnp.logical_not(early_cross(far - k)), across, 2)),
+            )
 
         @pl.when(far + k < depth)
         def _():
             owner = at(far + k, side, core)
-            arrived(owner)
-            pl.when(has_below)(lambda: send(owner, below, 1))
-            pl.when(jnp.logical_not(early_cross(far + k)))(lambda: send(owner, across, 2))
-            send(owner, twin, 3)
+            relay(
+                owner,
+                ((has_below, below, 1), (jnp.logical_not(early_cross(far + k)), across, 2)),
+            )
 
         def from_across(z):
             owner = at(z, 1 - side, core)
-            arrived(owner)
-            pl.when(early_cross(z) & has_above & (z <= far))(lambda: send(owner, above, 0))
-            pl.when(early_cross(z) & has_below & (z >= far))(lambda: send(owner, below, 1))
-            send(owner, twin, 3)
+            relay(
+                owner,
+                (
+                    (early_cross(z) & has_above & (z <= far), above, 0),
+                    (early_cross(z) & has_below & (z >= far), below, 1),
+                ),
+            )
 
         last = k - 1
         behind = far - last >= 0
@@ -332,8 +352,8 @@
             pltpu.VMEM((index_heads * queries, head_width), jnp.bfloat16),
             pltpu.VMEM((index_heads * queries, LANES), jnp.float32),
             pltpu.VMEM((queries, LANES), jnp.int32),
-            pltpu.SemaphoreType.DMA((4, 3, members)),
-            pltpu.SemaphoreType.DMA((3, members)),
+            pltpu.SemaphoreType.DMA((4, 4, members)),
+            pltpu.SemaphoreType.DMA((4, members)),
         ],
         compiler_params=pltpu.CompilerParams(
             collective_id=0, has_side_effects=True, vmem_limit_bytes=60 * 2**20

time: 56.2 us -> 53.4 us (0.950)
  Pallas kernels: 55.4 us -> 52.6 us
    pallas_call x1, Pallas kernels: 43.7 us -> 41 us  [on_device(): pl.pallas_call(functools.partial(exchange_kernel, members, index_heads, 1...]
where the time goes in v5:
time: 53.4 us; the launch traced here: 53.3 us
  Pallas kernels  52.6 us (99%)
  between operations  0.64 us (1%)
    pallas_call x1, Pallas kernels, on_device(): pl.pallas_call(functools.partial(exchange_kernel, members, index_heads, 1...  41 us
    pallas_call x1, Pallas kernels, on_device(): pl.pallas_call(attend_kernel, grid=(steps,), out_shape=(jax.ShapeDtypeStr...  11.7 us

profile of v5, /device:TPU:1, one launch (start us, length us, event | category | flops | bytes accessed | tf_op | source)
XLA Modules:
  0.0 53.3 jit_solution(8385003802312352852)
XLA Ops:
  0.6 41.0 %exchange.1 = (f32[16,4096]{1,0:T(8,128)}, bf16[576,1280]{1,0:T(8,128)(2,1)}, f32[16,1280]{1,0:T(8,128)}, f32[256,576]{1,0:T(8,128)}, f32[256,128]{1,0:T(8,128)}) custom-call(bf16[576,256]{1,0:T(8,128)(2,1)} %bitcast.4, bf16[256,128]{1,0:T(8,128)(2,1)} %index_ref.1, s32[1,64]{1,0:T(1,128)} %bitcast.5, s32[16,2048]{1,0:T(8,128)} %keys_ref.1, s32[16]{0:T(128)} %count_ref.1, ...), custom_call_target="tpu_custom_call" | custom-call | tf_op jit(solution)/shard_map/exchange/pallas_call | solution.py:335
  41.6 11.7 %attend.1 = (bf16[16,128,512]{2,1,0:T(8,128)(2,1)}, f32[16,4096]{1,0:T(8,128)}, bf16[64,4,576]{2,1,0:T(4,128)(2,1)}, bf16[64,4,128]{2,1,0:T(4,128)(2,1)}) custom-call(f32[16,1280]{1,0:T(8,128)} %get-tuple-element.13.bias_ref, bf16[16,576,128]{2,1,0:T(8,128)(2,1)} %bitcast.3, bf16[576,1280]{1,0:T(8,128)(2,1)} %get-tuple-element.14.chosen_ref, ...), custom_call_target="tpu_custom_call" | custom-call | tf_op jit(solution)/shard_map/attend/pallas_call | solution.py:370
